TPU v7x, 128 devices: a whole 4x4x4 slice. The times are simulated.
128 devices in a mesh: dp: 16 (over z, y_hi, core), expert: 8 (over y_lo, x).
Axes of the slice: x: 4, y: 4 (y_hi: 2, y_lo: 2; y = y_hi * 2 + y_lo), z: 4, core: 2. Of those that a mesh axis runs over, the one named last changes fastest.
Arguments:
- tokens: bfloat16 [1536, 6144], P(('dp', 'expert')), may hold values from -6 to 6
- cotangent: bfloat16 [1536, 6144], P(('dp', 'expert')), may hold values from -6 to 6
- expert_ids: int32 [1536, 2], P('dp'), may hold values from 0 to 7, all different within a row; in each aligned block of 96 rows (0 to 95, 96 to 191, ...) at most 32 rows name the same one
- gate_values: float32 [1536, 2], P('dp'), may hold values from 0.2 to 1
- w_in: bfloat16 [8, 6144, 8192], P('expert', None, 'dp'), may hold values from -0.078125 to 0.078125
- w_out: bfloat16 [8, 8192, 6144], P('expert', 'dp'), may hold values from -0.0625 to 0.0625
Outputs:
- layer_out: bfloat16 [1536, 6144], P(('dp', 'expert'))
- grad_tokens: bfloat16 [1536, 6144], P(('dp', 'expert'))
- grad_in: bfloat16 [8, 6144, 8192], P('expert', None, 'dp')
- grad_out: bfloat16 [8, 8192, 6144], P('expert', 'dp')
Inputs may be any that keep to these rules, and one draw needn't show every extreme that they name: `expert_ids`: A token names 2 different experts. Within the 96 tokens of one dp index no expert is named by more than 32 tokens, and in every draw some expert is named by exactly 32 tokens of some dp index.
All inputs are finite; a program needn't handle non-finite values.
Results may differ from a plain program's by a relative error of at most 0.0058.
Values may be sent and summed in bfloat16 or wider, within the bound.
A program may use at most 192 MiB of HBM per device.

v0:
```python
import jax
import jax.numpy as jnp
from jax import lax
from jax.sharding import PartitionSpec as P


def slot_tables(ids, gates, expert, slot_count):
    chosen = ids == expert
    gate_sum = jnp.sum(jnp.where(chosen, gates, jnp.float32(0.0)), axis=1)
    picked = jnp.any(chosen, axis=1).astype(jnp.int32)
    placed = jnp.cumsum(picked) - 1
    slots = lax.broadcasted_iota(jnp.int32, (slot_count, ids.shape[0]), 0)
    table = ((placed[None, :] == slots) & (picked[None, :] == 1)).astype(jnp.float32)
    return (table, gate_sum)


def unpack(table, slot_rows):
    return jnp.dot(
        table.T, slot_rows, precision=lax.Precision.HIGHEST, preferred_element_type=jnp.float32
    )


def local(tokens, cotangent, expert_ids, gate_values, w_in, w_out):
    group_tokens = expert_ids.shape[0]
    slot_count = max(
        group_tokens // 3, expert_ids.shape[1] * group_tokens // lax.axis_size("expert")
    )
    expert = lax.axis_index("expert")
    table, gate_sum = slot_tables(expert_ids, gate_values, expert, slot_count)
    table_half = table.astype(jnp.bfloat16)
    weight_in = w_in[0]
    weight_out = w_out[0]
    group_in, group_cot = (
        lax.all_gather(tokens, "expert", axis=0, tiled=True),
        lax.all_gather(cotangent, "expert", axis=0, tiled=True),
    )
    packed = jnp.dot(table_half, group_in, preferred_element_type=jnp.float32).astype(jnp.bfloat16)
    rows = lax.all_gather(packed, "dp", axis=0, tiled=True)
    pre = jnp.dot(rows, weight_in, preferred_element_type=jnp.float32)
    hidden = jax.nn.silu(pre).astype(jnp.bfloat16)
    weighted = (gate_sum[:, None] * group_cot).astype(jnp.bfloat16)
    packed_grad = jnp.dot(table_half, weighted, preferred_element_type=jnp.float32).astype(
        jnp.bfloat16
    )
    piece = hidden
    slot_out = lax.psum_scatter(
        jnp.dot(piece, weight_out, preferred_element_type=jnp.float32),
        "dp",
        scatter_dimension=0,
        tiled=True,
    )
    out_term = gate_sum[:, None] * unpack(table, slot_out)
    layer_out = lax.psum_scatter(out_term, "expert", scatter_dimension=0, tiled=True).astype(
        jnp.bfloat16
    )
    row_keep, slot_grad = (
        lax.all_gather(packed, "dp", axis=0, tiled=True),
        lax.all_gather(packed_grad, "dp", axis=0, tiled=True),
    )
    grad_out = jnp.einsum("rf,rd->fd", hidden, slot_grad, preferred_element_type=jnp.float32)
    grad_hidden = jnp.einsum("rd,fd->rf", slot_grad, weight_out, preferred_element_type=jnp.float32)
    sig = jax.nn.sigmoid(pre)
    grad_pre = (grad_hidden * sig * (1.0 + pre * (1.0 - sig))).astype(jnp.bfloat16)
    grad_in = jnp.einsum("rd,rf->df", row_keep, grad_pre, preferred_element_type=jnp.float32)
    piece = grad_pre
    slot_back = lax.psum_scatter(
        jnp.einsum("rf,df->rd", piece, weight_in, preferred_element_type=jnp.float32),
        "dp",
        scatter_dimension=0,
        tiled=True,
    )
    back_term = unpack(table, slot_back)
    grad_tokens = lax.psum_scatter(back_term, "expert", scatter_dimension=0, tiled=True).astype(
        jnp.bfloat16
    )
    return (
        layer_out,
        grad_tokens,
        grad_in.astype(jnp.bfloat16)[None],
        grad_out.astype(jnp.bfloat16)[None],
    )


def solution(mesh):
    placed = (
        P(("dp", "expert"), None),
        P(("dp", "expert"), None),
        P("dp", None),
        P("dp", None),
        P("expert", None, "dp"),
        P("expert", "dp", None),
    )
    return jax.shard_map(
        local,
        mesh=mesh,
        in_specs=placed,
        out_specs=(
            P(("dp", "expert"), None),
            P(("dp", "expert"), None),
            P("expert", None, "dp"),
            P("expert", "dp", None),
        ),
        check_vma=False,
    )
```

profile of v0, /device:TPU:4, one launch (start us, length us, event | category | flops | bytes accessed | tf_op | source)
XLA Modules:
  0.0 590.6 jit_solution(5294595046763693529)
XLA Ops:
  7.2 0.0 all-gather.11.cloned.1.call-start
  7.2 0.7 all-gather.11.cloned.1.call-update
  7.9 0.0 all-gather.13.cloned.1.call-start
  7.9 0.7 all-gather.13.cloned.1.call-update
  8.6 0.0 all-gather.7.cloned.1.call-start
  8.7 0.7 fusion.34
  9.4 0.1 copy.12
  9.5 0.1 reduce-window.8
  9.7 0.1 add_reduce_fusion
  9.8 40.8 %all-gather.11.cloned.1.call-done = bf16[8,12,6144]{2,1,0:T(8,128)(2,1)} async-done(((bf16[1,12,6144]{2,1,0:T(8,128)(2,1)}), bf16[8,12,6144]{2,1,0:T(8,128)(2,1)}) %all-gather.11.cloned.1.call-update) | async-done | bytes 1179664 | tf_op jit(solution)/shard_map/all_gather | solution.py:34
  50.5 1.5 reshape.48
  52.1 1.0 convolution_convert_fusion.3
  53.1 0.0 all-gather.7.cloned.1.call-update
  53.1 0.0 all-gather.9.cloned.1.call-start
  53.2 0.7 select_reduce_fusion
  53.9 38.0 %all-gather.13.cloned.1.call-done = bf16[8,12,6144]{2,1,0:T(8,128)(2,1)} async-done(((bf16[1,12,6144]{2,1,0:T(8,128)(2,1)}), bf16[8,12,6144]{2,1,0:T(8,128)(2,1)}) %all-gather.13.cloned.1.call-update) | async-done | bytes 1179664 | tf_op jit(solution)/shard_map/all_gather | solution.py:35
  92.0 1.5 reshape.51
  93.5 1.1 convolution_convert_fusion.2
  94.6 0.0 all-gather.9.cloned.1.call-update
  94.6 0.0 reduce-scatter.7.cloned.1.call-start
  94.7 65.8 %all-gather.7.cloned.1.call-done = bf16[512,6144]{1,0:T(8,128)(2,1)} async-done(((bf16[32,6144]{1,0:T(8,128)(2,1)}), bf16[512,6144]{1,0:T(8,128)(2,1)}) %all-gather.7.cloned.1.call-update) | async-done | bytes 6291472 | tf_op jit(solution)/shard_map/all_gather | solution.py:38
  160.5 7.5 %fusion.10 = f32[512,512]{1,0:T(8,128)S(1)} fusion(bf16[512,6144]{1,0:T(8,128)(2,1)} %all-gather.7.cloned.1.call-done, bf16[1,6144,512]{2,1,0:T(8,128)(2,1)} %param.10), kind=kOutput, calls=%fused_computation.13 | convolution fusion | flops 3221225472 | bytes 13631488 | tf_op jit(solution)/shard_map/dot_general | solution.py:39
  168.0 9.2 %fusion.6 = f32[512,6144]{1,0:T(8,128)} fusion(bf16[1,512,6144]{2,1,0:T(8,128)(2,1)} %param.11, f32[512,512]{1,0:T(8,128)S(1)} %fusion.10), kind=kOutput, calls=%fused_computation.9 | convolution fusion | flops 3222536192 | bytes 19922944 | tf_op jit(solution)/shard_map/dot_general | solution.py:47
  177.2 0.2 reduce-scatter.9.cloned.1.call-start
  177.5 47.9 %all-gather.9.cloned.1.call-done = bf16[512,6144]{1,0:T(8,128)(2,1)} async-done(((bf16[32,6144]{1,0:T(8,128)(2,1)}), bf16[512,6144]{1,0:T(8,128)(2,1)}) %all-gather.9.cloned.1.call-update) | async-done | bytes 6291472 | tf_op jit(solution)/shard_map/all_gather | solution.py:58
  225.4 8.2 %fusion.18 = bf16[512,512]{1,0:T(8,128)(2,1)S(1)} fusion(bf16[512,6144]{1,0:T(8,128)(2,1)} %all-gather.9.cloned.1.call-done, bf16[1,512,6144]{2,1,0:T(8,128)(2,1)} %param.11, f32[512,512]{1,0:T(8,128)S(1)} %fusion.10), kind=kOutput, calls=%fused_computation.18 | convolution fusion | flops 3223584768 | bytes 14155776 | tf_op jit(solution)/shard_map/rd,fd->rf/dot_general | solution.py:61
  233.6 11.0 %fusion.8 = f32[512,6144]{1,0:T(8,128)} fusion(bf16[512,512]{1,0:T(8,128)(2,1)S(1)} %fusion.18, bf16[1,6144,512]{2,1,0:T(8,128)(2,1)} %param.10), kind=kOutput, calls=%fused_computation.11 | convolution fusion | flops 3221225472 | bytes 19398656 | tf_op jit(solution)/shard_map/rf,df->rd/dot_general | solution.py:67
  244.6 0.0 reduce-scatter.9.cloned.1.call-update
  244.6 0.6 copy-done.2
  245.3 0.6 dynamic-slice.6
  246.5 9.1 %fusion.2 = bf16[1,6144,512]{2,1,0:T(8,128)(2,1)} fusion(bf16[512,6144]{1,0:T(8,128)(2,1)} %all-gather.7.cloned.1.call-done, bf16[512,512]{1,0:T(8,128)(2,1)S(1)} %fusion.18), kind=kOutput, calls=%fused_computation.2 | convolution fusion | flops 3224371200 | bytes 13107200 | tf_op jit(solution)/shard_map/rd,rf->df/dot_general | solution.py:64
  255.6 94.1 %reduce-scatter.7.cloned.1.call-done = f32[32,6144]{1,0:T(8,128)} async-done(((f32[512,6144]{1,0:T(8,128)}), f32[32,6144]{1,0:T(8,128)}) %reduce-scatter.7.cloned.1.call-update) | async-done | bytes 786448 | tf_op jit(solution)/shard_map/reduce_scatter | solution.py:46
  349.7 2.3 convolution_multiply_fusion
  352.0 122.6 %reduce-scatter.9.cloned.1.call-done = f32[32,6144]{1,0:T(8,128)} async-done(((f32[512,6144]{1,0:T(8,128)}), f32[32,6144]{1,0:T(8,128)}) %reduce-scatter.9.cloned.1.call-update) | async-done | bytes 786448 | tf_op jit(solution)/shard_map/reduce_scatter | solution.py:66
  474.6 3.7 fusion.23
  478.3 72.7 %fusion.35 = (f32[16,6144]{1,0:T(8,128)}, f32[16,6144]{1,0:T(8,128)}) fusion(f32[96,6144]{1,0:T(8,128)S(1)} %convolution_multiply_fusion, f32[96,6144]{1,0:T(8,128)} %fusion.23), kind=kCustom, calls=%all-reduce-scatter.2 | all-reduce-scatter fusion | flops 1572865 | bytes 5505536
  551.0 1.0 slice.1
  552.0 1.0 convert.2
  553.0 2.6 collective-permute-start.2
  555.7 5.5 collective-permute-start.3
  561.2 8.2 %fusion.3 = bf16[1,512,6144]{2,1,0:T(8,128)(2,1)} fusion(bf16[512,6144]{1,0:T(8,128)(2,1)} %all-gather.9.cloned.1.call-done, f32[512,512]{1,0:T(8,128)S(1)} %fusion.10), kind=kOutput, calls=%fused_computation.3 | convolution fusion | flops 3225681920 | bytes 13631488 | tf_op jit(solution)/shard_map/rf,rd->fd/dot_general | solution.py:60
  569.5 2.5 collective-permute-start
  572.0 1.9 collective-permute-start.1
  574.0 1.1 concatenate.1
  575.0 0.7 dynamic-slice_convert_fusion
  575.8 6.2 %collective-permute-done.1 = bf16[12,6144]{1,0:T(8,128)(2,1)S(1)} collective-permute-done((bf16[12,6144]{1,0:T(8,128)(2,1)S(1)}, bf16[12,6144]{1,0:T(8,128)(2,1)S(1)}, u32[]{:S(2)}, u32[]{:S(2)}) %collective-permute-start.1) | collective-permute-done | bytes 147488
  582.0 1.1 concatenate
  583.0 0.7 dynamic-slice_convert_fusion.1
  (12 shorter events, 0.1 us)
Async XLA Ops:
  7.2 43.4 %all-gather.11.cloned.1.call-start = ((), (), s32[]{:S(2)}) async-start(), calls=%async_computation.6 | async-start | bytes 1769472 | tf_op jit(solution)/shard_map/all_gather | solution.py:34
  7.9 84.1 %all-gather.13.cloned.1.call-start = ((), (), s32[]{:S(2)}) async-start(), calls=%async_computation.7 | async-start | bytes 1769472 | tf_op jit(solution)/shard_map/all_gather | solution.py:35
  8.6 151.9 %all-gather.7.cloned.1.call-start = ((), (), s32[]{:S(2)}) async-start(), calls=%async_computation.2 | async-start | bytes 6684672 | tf_op jit(solution)/shard_map/all_gather | solution.py:38
  53.1 172.2 %all-gather.9.cloned.1.call-start = ((), (), s32[]{:S(2)}) async-start(), calls=%async_computation.4 | async-start | bytes 6684672 | tf_op jit(solution)/shard_map/all_gather | solution.py:58
  94.6 255.1 %reduce-scatter.7.cloned.1.call-start = ((), (), s32[]{:S(2)}) async-start(), calls=%async_computation.3 | async-start | bytes 13369344 | tf_op jit(solution)/shard_map/reduce_scatter | solution.py:46
  177.2 297.4 %reduce-scatter.9.cloned.1.call-start = ((), (), s32[]{:S(2)}) async-start(), calls=%async_computation.5 | async-start | bytes 13369344 | tf_op jit(solution)/shard_map/reduce_scatter | solution.py:66
  244.6 0.7 copy-start.2
  553.0 16.4 %copy-start = (f32[16,6144]{1,0:T(8,128)S(1)}, f32[16,6144]{1,0:T(8,128)}, u32[]{:S(2)}) copy-start(f32[16,6144]{1,0:T(8,128)} %get-tuple-element.6) | copy-start | bytes 1179652
  553.0 20.9 %copy-start.1 = (f32[16,6144]{1,0:T(8,128)S(1)}, f32[16,6144]{1,0:T(8,128)}, u32[]{:S(2)}) copy-start(f32[16,6144]{1,0:T(8,128)} %get-tuple-element.7) | copy-start | bytes 1179652
  553.0 20.9 %collective-permute-start.2 = (bf16[16,6144]{1,0:T(8,128)(2,1)S(1)}, bf16[16,6144]{1,0:T(8,128)(2,1)S(1)}, u32[]{:S(2)}, u32[]{:S(2)}) collective-permute-start(bf16[16,6144]{1,0:T(8,128)(2,1)S(1)} %convert.2), channel_id=1, source_target_pairs={{0,1},{1,2},{2,3},{3,4},{4,5},{5,6},{6,7},{8,9},{9,10},{10,11},{11... | collective-permute-start | bytes 589832
  555.7 18.2 %collective-permute-start.3 = (bf16[12,6144]{1,0:T(8,128)(2,1)S(1)}, bf16[12,6144]{1,0:T(8,128)(2,1)S(1)}, u32[]{:S(2)}, u32[]{:S(2)}) collective-permute-start(bf16[12,6144]{1,0:T(8,128)(2,1)S(1)} %slice.1), channel_id=1, source_target_pairs={{0,2},{1,3},{2,4},{3,5},{4,6},{5,7},{8,10},{9,11},{10,12},{11,13},... | collective-permute-start | bytes 442376
  569.5 12.5 %collective-permute-start = (bf16[16,6144]{1,0:T(8,128)(2,1)S(1)}, bf16[16,6144]{1,0:T(8,128)(2,1)S(1)}, u32[]{:S(2)}, u32[]{:S(2)}) collective-permute-start(bf16[16,6144]{1,0:T(8,128)(2,1)S(1)} %convert.1), channel_id=1, source_target_pairs={{0,1},{1,2},{2,3},{3,4},{4,5},{5,6},{6,7},{8,9},{9,10},{10,11},{11... | collective-permute-start | bytes 589832
  572.0 9.9 %collective-permute-start.1 = (bf16[12,6144]{1,0:T(8,128)(2,1)S(1)}, bf16[12,6144]{1,0:T(8,128)(2,1)S(1)}, u32[]{:S(2)}, u32[]{:S(2)}) collective-permute-start(bf16[12,6144]{1,0:T(8,128)(2,1)S(1)} %slice), channel_id=1, source_target_pairs={{0,2},{1,3},{2,4},{3,5},{4,6},{5,7},{8,10},{9,11},{10,12},{11,13},... | collective-permute-start | bytes 442376
Sparse Core Ops, SparseCore 0:
  9.6 40.8 all-gather.10
  52.2 39.7 all-gather.12
  95.0 65.4 all-gather.6
  163.4 61.9 all-gather.8
  229.5 120.1 reduce-scatter.6
  353.9 120.6 reduce-scatter.8
where the time goes:
time: 591 us
  waiting for transfers between devices  417 us (71%)
  blocking collectives  72.7 us (12%)
  matrix products  61.3 us (10%)
  between operations  14.9 us (3%)
  starting transfers between devices  13 us (2%)
  local copies, waits for them, and re-layouts  9.03 us (2%)
    reduce_scatter x1, waiting for transfers between devices, local(): lax.psum_scatter(jnp.einsum('rf,df->rd', piece, weight_in, preferred_elem...  123 us
    reduce_scatter x1, waiting for transfers between devices, local(): lax.psum_scatter(jnp.dot(piece, weight_out, preferred_element_type=jnp.fl...  94.1 us
    unnamed x1, blocking collectives  72.7 us
    all_gather x1, waiting for transfers between devices, local(): rows = lax.all_gather(packed, 'dp', axis=0, tiled=True)  65.8 us
    all_gather x1, waiting for transfers between devices, local(): lax.all_gather(packed_grad, 'dp', axis=0, tiled=True)  47.9 us
    all_gather x1, waiting for transfers between devices, local(): lax.all_gather(tokens, 'expert', axis=0, tiled=True)  40.8 us
    all_gather x1, waiting for transfers between devices, local(): lax.all_gather(cotangent, 'expert', axis=0, tiled=True)  38 us
    unnamed x4, starting transfers between devices  12.6 us
  transfers between devices with their start and end apart: 10, of which 7 were waited for; matrix products, arithmetic and copies ran while one was open for 11% of the time, Pallas kernels for 0%

commit v1 on v0

--- a/solution.py
+++ b/solution.py
@@ -2,6 +2,16 @@
 import jax.numpy as jnp
 from jax import lax
 from jax.sharding import PartitionSpec as P
+
+
+def wait_pages(z):
+    top = jnp.concatenate(
+        lax.all_to_all(
+            jnp.stack(lax.axis_size("dp") * [z]), concat_axis=0, axis_name="dp", split_axis=0
+        ),
+        axis=0,
+    )
+    return top
 
 
 def slot_tables(ids, gates, expert, slot_count):
@@ -35,7 +45,7 @@
         lax.all_gather(cotangent, "expert", axis=0, tiled=True),
     )
     packed = jnp.dot(table_half, group_in, preferred_element_type=jnp.float32).astype(jnp.bfloat16)
-    rows = lax.all_gather(packed, "dp", axis=0, tiled=True)
+    rows = wait_pages(packed)
     pre = jnp.dot(rows, weight_in, preferred_element_type=jnp.float32)
     hidden = jax.nn.silu(pre).astype(jnp.bfloat16)
     weighted = (gate_sum[:, None] * group_cot).astype(jnp.bfloat16)

time: 591 us -> 633 us (1.071)
  blocking collectives: 72.7 us -> 175 us
  waiting for transfers between devices: 417 us -> 364 us
  matrix products: 61.3 us -> 52.1 us
    all_to_all x0 -> x1, blocking collectives: none -> 102 us  [wait_pages(): lax.all_to_all(jnp.stack(lax.axis_size('dp') * [z]), concat_axis=0, axis_...]
    all_gather x1, waiting for transfers between devices: 47.9 us -> 0.02 us  [local(): lax.all_gather(packed_grad, 'dp', axis=0, tiled=True)]
    all_gather x1, waiting for transfers between devices: 65.8 us -> 38.4 us  [local(): lax.all_gather(packed, 'dp', axis=0, tiled=True)]
    reduce_scatter x1, waiting for transfers between devices: 94.1 us -> 116 us  [local(): lax.psum_scatter(jnp.dot(piece, weight_out, preferred_element_type=jnp.fl...]
  transfers between devices with their start and end apart: 10 -> 10, of which waited for: 7 -> 7; matrix products, arithmetic and copies ran while one was open for 11% -> 9% of each run, Pallas kernels for 0% -> 0%
where the time goes in v1:
time: 633 us
  waiting for transfers between devices  364 us (58%)
  blocking collectives  175 us (28%)
  matrix products  52.1 us (8%)
  between operations  15 us (2%)
  starting transfers between devices  13 us (2%)
  local copies, waits for them, and re-layouts  10.9 us (2%)
    reduce_scatter x1, waiting for transfers between devices, local(): lax.psum_scatter(jnp.einsum('rf,df->rd', piece, weight_in, preferred_elem...  123 us
    reduce_scatter x1, waiting for transfers between devices, local(): lax.psum_scatter(jnp.dot(piece, weight_out, preferred_element_type=jnp.fl...  116 us
    all_to_all x1, blocking collectives, wait_pages(): lax.all_to_all(jnp.stack(lax.axis_size('dp') * [z]), concat_axis=0, axis_...  102 us
    unnamed x1, blocking collectives  72.7 us
    all_gather x1, waiting for transfers between devices, local(): lax.all_gather(cotangent, 'expert', axis=0, tiled=True)  40.1 us
    all_gather x1, waiting for transfers between devices, local(): lax.all_gather(tokens, 'expert', axis=0, tiled=True)  38.7 us
    all_gather x1, waiting for transfers between devices, local(): lax.all_gather(packed, 'dp', axis=0, tiled=True)  38.4 us
  transfers between devices with their start and end apart: 10, of which 7 were waited for; matrix products, arithmetic and copies ran while one was open for 9% of the time, Pallas kernels for 0%

profile of v1, /device:TPU:4, one launch (start us, length us, event | category | flops | bytes accessed | tf_op | source)
XLA Modules:
  0.0 632.6 jit_solution(17623139273616379257)
XLA Ops:
  7.2 0.0 all-gather.13.cloned.1.call-start
  7.2 0.7 all-gather.13.cloned.1.call-update
  7.9 0.0 all-gather.11.cloned.1.call-start
  7.9 0.7 all-gather.11.cloned.1.call-update
  8.6 0.0 all-gather.7.cloned.1.call-start
  8.7 0.7 fusion.34
  9.4 0.1 copy.12
  9.5 0.1 reduce-window.8
  9.7 0.7 select_reduce_fusion
  10.4 0.1 add_reduce_fusion
  10.5 40.1 %all-gather.13.cloned.1.call-done = bf16[8,12,6144]{2,1,0:T(8,128)(2,1)} async-done(((bf16[1,12,6144]{2,1,0:T(8,128)(2,1)}), bf16[8,12,6144]{2,1,0:T(8,128)(2,1)}) %all-gather.13.cloned.1.call-update) | async-done | bytes 1179664 | tf_op jit(solution)/shard_map/all_gather | solution.py:45
  50.5 1.5 reshape.57
  52.1 1.1 convolution_convert_fusion.2
  53.2 0.0 all-gather.9.cloned.1.call-start
  53.3 38.7 %all-gather.11.cloned.1.call-done = bf16[8,12,6144]{2,1,0:T(8,128)(2,1)} async-done(((bf16[1,12,6144]{2,1,0:T(8,128)(2,1)}), bf16[8,12,6144]{2,1,0:T(8,128)(2,1)}) %all-gather.11.cloned.1.call-update) | async-done | bytes 1179664 | tf_op jit(solution)/shard_map/all_gather | solution.py:44
  92.0 1.5 reshape.54
  93.5 1.0 convolution_convert_fusion.3
  94.6 0.0 reduce-scatter.7.cloned.1.call-start
  94.6 1.9 stack.2
  96.6 102.3 %all_to_all.5 = bf16[16,32,6144]{2,1,0:T(8,128)(2,1)S(1)} all-to-all(bf16[16,32,6144]{2,1,0:T(8,128)(2,1)S(1)} %stack.2), channel_id=1, replica_groups=mesh['dp'=16,'expert'=8] {'dp'}, dimensions={0} | all-to-all | bytes 12582912 | tf_op jit(solution)/shard_map/all_to_all | solution.py:9
  198.8 3.4 fusion.10
  202.3 6.5 %fusion.6 = f32[512,6144]{1,0:T(8,128)} fusion(bf16[1,512,6144]{2,1,0:T(8,128)(2,1)S(1)} %bitcast.41, f32[512,512]{1,0:T(8,128)S(1)} %fusion.10), kind=kOutput, calls=%fused_computation.9 | convolution fusion | flops 3222536192 | bytes 19922944 | tf_op jit(solution)/shard_map/dot_general | solution.py:57
  208.8 0.2 reduce-scatter.9.cloned.1.call-start
  209.0 0.0 all-gather.7.cloned.1.call-done
  209.0 8.5 %fusion.18 = bf16[512,512]{1,0:T(8,128)(2,1)S(1)} fusion(bf16[512,6144]{1,0:T(8,128)(2,1)} %all-gather.7.cloned.1.call-done, bf16[1,512,6144]{2,1,0:T(8,128)(2,1)} %param.11, f32[512,512]{1,0:T(8,128)S(1)} %fusion.10), kind=kOutput, calls=%fused_computation.18 | convolution fusion | flops 3223584768 | bytes 14155776 | tf_op jit(solution)/shard_map/rd,fd->rf/dot_general | solution.py:71
  217.5 9.2 %fusion.8 = f32[512,6144]{1,0:T(8,128)} fusion(bf16[512,512]{1,0:T(8,128)(2,1)S(1)} %fusion.18, bf16[1,6144,512]{2,1,0:T(8,128)(2,1)} %param.10), kind=kOutput, calls=%fused_computation.11 | convolution fusion | flops 3221225472 | bytes 19398656 | tf_op jit(solution)/shard_map/rf,df->rd/dot_general | solution.py:77
  226.7 0.6 copy-done.2
  227.3 0.6 dynamic-slice.6
  228.6 38.4 %all-gather.9.cloned.1.call-done = bf16[512,6144]{1,0:T(8,128)(2,1)} async-done(((bf16[32,6144]{1,0:T(8,128)(2,1)}), bf16[512,6144]{1,0:T(8,128)(2,1)}) %all-gather.9.cloned.1.call-update) | async-done | bytes 6291472 | tf_op jit(solution)/shard_map/all_gather | solution.py:67
  267.0 8.2 %fusion.2 = bf16[1,6144,512]{2,1,0:T(8,128)(2,1)} fusion(bf16[512,6144]{1,0:T(8,128)(2,1)} %all-gather.9.cloned.1.call-done, bf16[512,512]{1,0:T(8,128)(2,1)S(1)} %fusion.18), kind=kOutput, calls=%fused_computation.2 | convolution fusion | flops 3224371200 | bytes 13107200 | tf_op jit(solution)/shard_map/rd,rf->df/dot_general | solution.py:74
  275.2 116.2 %reduce-scatter.7.cloned.1.call-done = f32[32,6144]{1,0:T(8,128)} async-done(((f32[512,6144]{1,0:T(8,128)}), f32[32,6144]{1,0:T(8,128)}) %reduce-scatter.7.cloned.1.call-update) | async-done | bytes 786448 | tf_op jit(solution)/shard_map/reduce_scatter | solution.py:56
  391.3 2.3 convolution_multiply_fusion
  393.6 122.6 %reduce-scatter.9.cloned.1.call-done = f32[32,6144]{1,0:T(8,128)} async-done(((f32[512,6144]{1,0:T(8,128)}), f32[32,6144]{1,0:T(8,128)}) %reduce-scatter.9.cloned.1.call-update) | async-done | bytes 786448 | tf_op jit(solution)/shard_map/reduce_scatter | solution.py:76
  516.2 3.7 fusion.23
  519.9 72.7 %fusion.35 = (f32[16,6144]{1,0:T(8,128)}, f32[16,6144]{1,0:T(8,128)}) fusion(f32[96,6144]{1,0:T(8,128)S(1)} %convolution_multiply_fusion, f32[96,6144]{1,0:T(8,128)} %fusion.23), kind=kCustom, calls=%all-reduce-scatter.2 | all-reduce-scatter fusion | flops 1572865 | bytes 5505536
  592.6 1.0 slice
  593.6 1.0 convert.1
  594.7 4.8 collective-permute-start.1
  599.5 3.9 collective-permute-start
  603.4 8.2 %fusion.3 = bf16[1,512,6144]{2,1,0:T(8,128)(2,1)} fusion(bf16[512,6144]{1,0:T(8,128)(2,1)} %all-gather.7.cloned.1.call-done, f32[512,512]{1,0:T(8,128)S(1)} %fusion.10), kind=kOutput, calls=%fused_computation.3 | convolution fusion | flops 3225681920 | bytes 13631488 | tf_op jit(solution)/shard_map/rf,rd->fd/dot_general | solution.py:70
  611.7 1.9 collective-permute-start.3
  613.6 1.9 collective-permute-start.2
  615.6 1.1 concatenate
  616.7 0.7 dynamic-slice_convert_fusion.1
  617.4 4.5 collective-permute-done.3
  621.9 2.0 collective-permute-done.2
  623.9 1.1 concatenate.1
  625.0 0.7 dynamic-slice_convert_fusion
  (24 shorter events, 0.2 us)
Async XLA Ops:
  7.2 43.4 %all-gather.13.cloned.1.call-start = ((), (), s32[]{:S(2)}) async-start(), calls=%async_computation.8 | async-start | bytes 1769472 | tf_op jit(solution)/shard_map/all_gather | solution.py:45
  7.9 84.1 %all-gather.11.cloned.1.call-start = ((), (), s32[]{:S(2)}) async-start(), calls=%async_computation.7 | async-start | bytes 1769472 | tf_op jit(solution)/shard_map/all_gather | solution.py:44
  8.6 200.4 %all-gather.7.cloned.1.call-start = ((), (), s32[]{:S(2)}) async-start(), calls=%async_computation.4 | async-start | bytes 6684672 | tf_op jit(solution)/shard_map/all_gather | solution.py:68
  53.2 213.8 %all-gather.9.cloned.1.call-start = ((), (), s32[]{:S(2)}) async-start(), calls=%async_computation.6 | async-start | bytes 6684672 | tf_op jit(solution)/shard_map/all_gather | solution.py:67
  94.6 296.8 %reduce-scatter.7.cloned.1.call-start = ((), (), s32[]{:S(2)}) async-start(), calls=%async_computation.3 | async-start | bytes 13369344 | tf_op jit(solution)/shard_map/reduce_scatter | solution.py:56
  94.6 104.2 %slice-start.2 = ((s8[6291456]{0:T(1024)(128)(4,1)}), s8[4194304]{0:T(1024)(128)(4,1)S(1)}, s32[]{:S(2)}) async-start(s8[6291456]{0:T(1024)(128)(4,1)} %bitcast.43), calls=%async_computation.11 | async-start | bytes 8388608
  96.5 102.3 %slice-start.3 = ((s8[6291456]{0:T(1024)(128)(4,1)}), s8[2097152]{0:T(1024)(128)(4,1)S(1)}, s32[]{:S(2)}) async-start(s8[6291456]{0:T(1024)(128)(4,1)} %bitcast.43), calls=%async_computation.12 | async-start | bytes 4194304
  96.5 105.7 %slice-start = ((s8[6291456]{0:T(1024)(128)(4,1)}), s8[4194304]{0:T(1024)(128)(4,1)S(1)}, s32[]{:S(2)}) async-start(s8[6291456]{0:T(1024)(128)(4,1)} %bitcast.40), calls=%async_computation.9 | async-start | bytes 8388608
  198.8 3.4 slice-start.1
  208.8 307.5 %reduce-scatter.9.cloned.1.call-start = ((), (), s32[]{:S(2)}) async-start(), calls=%async_computation.5 | async-start | bytes 13369344 | tf_op jit(solution)/shard_map/reduce_scatter | solution.py:76
  226.7 0.7 copy-start.2
  594.7 17.0 %copy-start = (f32[16,6144]{1,0:T(8,128)S(1)}, f32[16,6144]{1,0:T(8,128)}, u32[]{:S(2)}) copy-start(f32[16,6144]{1,0:T(8,128)} %get-tuple-element.7) | copy-start | bytes 1179652
  594.7 20.9 %copy-start.1 = (f32[16,6144]{1,0:T(8,128)S(1)}, f32[16,6144]{1,0:T(8,128)}, u32[]{:S(2)}) copy-start(f32[16,6144]{1,0:T(8,128)} %get-tuple-element.6) | copy-start | bytes 1179652
  594.7 20.9 %collective-permute-start.1 = (bf16[12,6144]{1,0:T(8,128)(2,1)S(1)}, bf16[12,6144]{1,0:T(8,128)(2,1)S(1)}, u32[]{:S(2)}, u32[]{:S(2)}) collective-permute-start(bf16[12,6144]{1,0:T(8,128)(2,1)S(1)} %slice), channel_id=1, source_target_pairs={{0,2},{1,3},{2,4},{3,5},{4,6},{5,7},{8,10},{9,11},{10,12},{11,13},... | collective-permute-start | bytes 442376
  599.5 16.1 %collective-permute-start = (bf16[16,6144]{1,0:T(8,128)(2,1)S(1)}, bf16[16,6144]{1,0:T(8,128)(2,1)S(1)}, u32[]{:S(2)}, u32[]{:S(2)}) collective-permute-start(bf16[16,6144]{1,0:T(8,128)(2,1)S(1)} %convert.1), channel_id=1, source_target_pairs={{0,1},{1,2},{2,3},{3,4},{4,5},{5,6},{6,7},{8,9},{9,10},{10,11},{11... | collective-permute-start | bytes 589832
  611.7 10.2 %collective-permute-start.3 = (bf16[12,6144]{1,0:T(8,128)(2,1)S(1)}, bf16[12,6144]{1,0:T(8,128)(2,1)S(1)}, u32[]{:S(2)}, u32[]{:S(2)}) collective-permute-start(bf16[12,6144]{1,0:T(8,128)(2,1)S(1)} %slice.1), channel_id=1, source_target_pairs={{0,2},{1,3},{2,4},{3,5},{4,6},{5,7},{8,10},{9,11},{10,12},{11,13},... | collective-permute-start | bytes 442376
  613.6 10.3 %collective-permute-start.2 = (bf16[16,6144]{1,0:T(8,128)(2,1)S(1)}, bf16[16,6144]{1,0:T(8,128)(2,1)S(1)}, u32[]{:S(2)}, u32[]{:S(2)}) collective-permute-start(bf16[16,6144]{1,0:T(8,128)(2,1)S(1)} %convert.2), channel_id=1, source_target_pairs={{0,1},{1,2},{2,3},{3,4},{4,5},{5,6},{6,7},{8,9},{9,10},{10,11},{11... | collective-permute-start | bytes 589832
Sparse Core Ops, SparseCore 0:
  9.6 40.8 all-gather.12
  52.2 39.7 all-gather.10
  95.0 107.6 all-gather.6
  205.6 61.3 all-gather.8
  271.2 120.1 reduce-scatter.6
  395.5 120.6 reduce-scatter.8
